TPU v7x, 32 devices: a whole 2x2x4 slice. The times are simulated.
32 devices in a mesh: lat: 16 (over z, y, x), depth: 2 (over core).
Axes of the slice: x: 2, y: 2, z: 4, core: 2. Of those that a mesh axis runs over, the one named last changes fastest.
Arguments:
- saved_waves: float32 [2, 32, 2, 256, 256], P(None, 'lat', 'depth'), may hold values from -5 to 5
- object_slices: float32 [2, 2, 256, 4096], P(None, 'depth', None, 'lat'), may hold values from -5 to 5
- cotangent: float32 [2, 32, 256, 256], P(None, 'lat'), may hold values from -5 to 5
- transfer_phase: float32 [256, 256], replicated, may hold values from -3.140625 to 3.140625
- offsets: int32 [32], P('lat'), may hold values from 0 to 255
Outputs:
- object_grad: float32 [2, 2, 256, 4096], P(None, 'depth', None, 'lat')
- probe_grad: float32 [2, 256, 256], P(None, 'depth')
All inputs are finite; a program needn't handle non-finite values.
Results may differ from a plain program's by a relative error of at most 0.0003.
Values sent between devices are 32-bit elements; how exact they have to be, the bound alone decides.
A program may use at most 64 MiB of HBM per device.

v0:
```python
import math

import jax
import jax.numpy as jnp
from jax import lax
from jax.sharding import PartitionSpec as P


def from_behind(value, axis, steps):
    count = lax.axis_size(axis)
    pairs = [(source, (source + steps) % count) for source in range(count)]
    return lax.ppermute(value, axis, pairs)


def shifted(value, axis, steps):
    count = lax.axis_size(axis)
    first, last = (max(0, -steps), min(count, count - steps))
    return lax.ppermute(value, axis, [(source, source + steps) for source in range(first, last)])


def dft_tables(length):
    index = jnp.arange(length, dtype=jnp.int32)
    product = index[:, None] * index[None, :] % length
    angles = product.astype(jnp.float32) * (2.0 * math.pi / length)
    norm_scale = 1.0 / math.sqrt(length)
    return (jnp.cos(angles) * norm_scale, -jnp.sin(angles) * norm_scale)


def left_product(table, field):
    return jnp.einsum("jk,bkl->bjl", table, field, precision=lax.Precision.HIGHEST)


def right_product(table, field):
    return jnp.einsum("bjk,kl->bjl", field, table, precision=lax.Precision.HIGHEST)


def transform(tables, field_re, field_im, inverse):
    table_re, table_im = tables
    if inverse:
        table_im = -table_im
    half_re = left_product(table_re, field_re) - left_product(table_im, field_im)
    half_im = left_product(table_re, field_im) + left_product(table_im, field_re)
    full_re = right_product(table_re, half_re) - right_product(table_im, half_im)
    full_im = right_product(table_re, half_im) + right_product(table_im, half_re)
    return (full_re, full_im)


def adjoint_propagate(tables, phase_cos, phase_sin, field_re, field_im):
    spec_re, spec_im = transform(tables, field_re, field_im, False)
    turned_re = spec_re * phase_cos + spec_im * phase_sin
    turned_im = spec_im * phase_cos - spec_re * phase_sin
    return transform(tables, turned_re, turned_im, True)


def shards(saved_waves, object_slices, cotangent, transfer_phase, offsets):
    width = object_slices.shape[2]
    layers = object_slices.shape[1]
    positions = offsets.shape[0]
    batch = 1
    groups_count = positions // batch
    depth_size = lax.axis_size("depth")
    depth_index = lax.axis_index("depth")
    tables = dft_tables(width)
    phase_cos = jnp.cos(transfer_phase)
    phase_sin = jnp.sin(transfer_phase)
    neighbour = from_behind(object_slices, "lat", -1)
    window = jnp.concatenate([object_slices, neighbour], axis=3)

    def run_section(operands):
        wave_re, wave_im, grad_buffer, first = operands
        wave_block = lax.dynamic_slice_in_dim(saved_waves, first, batch, 1)
        shifts = lax.dynamic_slice_in_dim(offsets, first, batch, 0)
        patches = jnp.stack([lax.dynamic_slice_in_dim(window, shifts[0], width, 3)], axis=1)
        for layer in reversed(range(layers)):
            back_re, back_im = adjoint_propagate(tables, phase_cos, phase_sin, wave_re, wave_im)
            saved_re = wave_block[0, :, layer]
            saved_im = wave_block[1, :, layer]
            trans_re = patches[0, :, layer]
            trans_im = patches[1, :, layer]
            delta_re = saved_re * back_re + saved_im * back_im
            delta_im = saved_re * back_im - saved_im * back_re
            wave_re = trans_re * back_re + trans_im * back_im
            wave_im = trans_re * back_im - trans_im * back_re
            corner = (0, layer, 0, shifts[0])
            current = lax.dynamic_slice(grad_buffer, corner, (2, 1, width, width))
            addition = jnp.stack([delta_re[0], delta_im[0]])[:, None]
            grad_buffer = lax.dynamic_update_slice(grad_buffer, current + addition, corner)
        return (wave_re, wave_im, grad_buffer)

    def skip_section(operands):
        wave_re, wave_im, grad_buffer, first = operands
        return (jnp.zeros_like(wave_re), jnp.zeros_like(wave_im), grad_buffer)

    def tick(count, carry):
        received, grad_buffer, probe_sum = carry
        group = count - (depth_size - 1 - depth_index)
        active = (group >= 0) & (group < groups_count)
        first = jnp.clip(group, 0, groups_count - 1) * batch
        incoming = lax.dynamic_slice_in_dim(cotangent, first, batch, 1)
        entering = jnp.where(depth_index == depth_size - 1, incoming, received)
        wave_re, wave_im, grad_buffer = lax.cond(
            active, run_section, skip_section, (entering[0], entering[1], grad_buffer, first)
        )
        outgoing = jnp.stack([wave_re, wave_im])
        probe_sum = probe_sum + jnp.where(depth_index == 0, jnp.sum(outgoing, axis=1), 0.0)
        received = shifted(outgoing, "depth", -1)
        return (received, grad_buffer, probe_sum)

    initial = (
        jnp.zeros((2, batch, width, width), jnp.float32),
        jnp.zeros((2, layers, width, 2 * width), jnp.float32),
        jnp.zeros((2, width, width), jnp.float32),
    )
    ticks = groups_count + depth_size - 1
    received, grad_buffer, probe_sum = lax.fori_loop(0, ticks, tick, initial)
    overflow = from_behind(grad_buffer[..., width:], "lat", 1)
    object_grad = grad_buffer[..., :width] + overflow
    probe_band = lax.psum_scatter(probe_sum, "depth", scatter_dimension=1, tiled=True)
    probe_grad = lax.psum(probe_band, "lat")
    return (object_grad, probe_grad)


def solution(mesh):
    placed = (
        P(None, "lat", "depth", None, None),
        P(None, "depth", None, "lat"),
        P(None, "lat", None, None),
        P(),
        P("lat"),
    )
    return jax.shard_map(
        shards,
        mesh=mesh,
        in_specs=placed,
        out_specs=(P(None, "depth", None, "lat"), P(None, "depth", None)),
        check_vma=False,
    )
```

profile of v0, /device:TPU:0, one launch (start us, length us, event | category | flops | bytes accessed | tf_op | source)
XLA Modules:
  0.0 236.6 jit_solution(1438137076288583204)
XLA Ops:
  7.2 7.0 %collective-permute-start.1 = (f32[2,1,256,256]{3,2,1,0:T(8,128)}, f32[2,1,256,256]{3,2,1,0:T(8,128)S(1)}, u32[]{:S(2)}, u32[]{:S(2)}) collective-permute-start(f32[2,1,256,256]{3,2,1,0:T(8,128)} %param.10), channel_id=1, source_target_pairs={{0,30},{2,0},{4,2},{6,4},{8,6},{10,8},{12,10},{14,12},{16,14},{18,... | collective-permute-start | bytes 1572872 | tf_op jit(solution)/shard_map/ppermute | solution.py:12
  14.2 2.5 %fusion.22 = (f32[256,256]{1,0:T(8,128)S(1)}, f32[256,256]{1,0:T(8,128)}) fusion(f32[256,256]{1,0:T(8,128)} %param.12), kind=kLoop, calls=%fused_computation.51 | loop fusion | bytes 786432 | tf_op jit(solution)/shard_map/sin | solution.py:65
  16.7 9.0 %collective-permute-done.1 = f32[2,1,256,256]{3,2,1,0:T(8,128)S(1)} collective-permute-done((f32[2,1,256,256]{3,2,1,0:T(8,128)}, f32[2,1,256,256]{3,2,1,0:T(8,128)S(1)}, u32[]{:S(2)}, u32[]{:S(2)}) %collective-permute-start.1) | collective-permute-done | bytes 524320 | tf_op jit(solution)/shard_map/ppermute | solution.py:12
  25.7 1.1 pad_maximum_fusion.1
  27.0 0.6 copy-done.2
  27.6 75.9 %while.24 = (s32[]{:T(128)}, f32[2,1,256,256]{3,2,1,0:T(8,128)S(1)}, f32[2,1,256,512]{3,2,0,1:T(8,128)S(1)}, f32[2,256,256]{2,1,0:T(8,128)S(1)}, s32[]{:T(128)},...) while((s32[]{:T(128)}, ...), condition=%wide.region_3.4_spmd.clone.clone, body=%wide.region_0.3_spmd.clone.clone.sunk | while | flops 3225354240 | bytes 28836332 | solution.py:115
  27.9 1.3 collective-permute-start
  29.4 22.1 %collective-permute-done = f32[2,1,256,256]{3,2,0,1:T(8,128)S(1)} collective-permute-done((f32[2,1,256,256]{3,2,0,1:T(8,128)S(1)}, f32[2,1,256,256]{3,2,0,1:T(8,128)S(1)}, u32[]{:S(2)}, u32[]{:S(2)}) %collective-permute-start) | collective-permute-done | bytes 524320 | tf_op jit(solution)/shard_map/while/body/eval_jaxpr/ppermute | solution.py:18
  51.6 22.0 %conditional.4 = (f32[2,1,256,512]{3,2,0,1:T(8,128)S(1)}, f32[1,1,256,256]{3,2,1,0:T(8,128)S(1)}, f32[1,1,256,256]{3,2,1,0:T(8,128)S(1)}) conditional(s32[]{:T(128)} %convert_element_type.59, f32[2,1,256,512]{3,2,0,1:T(8,128)S(1)} %get-tuple-element.791, (s32[]{:T(128)}, s32[2]{0:T(128)S(1)}, f32[2,1,256,512]{3,2,0,1:T(8,128)S(1)}, ...), branch_computations={%region_1.1_spmd, %region_2.2_spmd.clone} | conditional | flops 3223781376 | bytes 23593088 | solution.py:101
  51.7 1.7 fusion.9
  53.4 1.1 dynamic-slice_select_fusion
  58.8 1.6 multiply_subtract_fusion
  64.0 0.6 convolution_add_fusion
  66.9 2.0 subtract_bitcast_fusion
  69.1 4.5 %dynamic_update_slice.5 = f32[2,1,256,512]{3,2,0,1:T(8,128)S(1)} dynamic-update-slice(f32[2,1,256,512]{3,2,0,1:T(8,128)S(1)} %get-tuple-element.615, f32[2,1,256,256]{3,2,0,1:T(8,128)S(1)} %fusion.8, s32[]{:T(128)} %constant.73.clone.1, s32[]{:T(128)} %constant.73.clone.1, s32[]{:T(128)} %constant.73.clone.1, s32[]{:T(128)S(6)} %select_n.117) | dynamic-update-slice | bytes 1048580 | tf_op jit(solution)/shard_map/while/body/eval_jaxpr/cond/branch_1_fun/dynamic_update_slice | solution.py:87
  73.7 1.3 collective-permute-start
  75.1 2.3 collective-permute-done
  77.6 22.0 %conditional.4 = (f32[2,1,256,512]{3,2,0,1:T(8,128)S(1)}, f32[1,1,256,256]{3,2,1,0:T(8,128)S(1)}, f32[1,1,256,256]{3,2,1,0:T(8,128)S(1)}) conditional(s32[]{:T(128)} %convert_element_type.59, f32[2,1,256,512]{3,2,0,1:T(8,128)S(1)} %get-tuple-element.791, (s32[]{:T(128)}, s32[2]{0:T(128)S(1)}, f32[2,1,256,512]{3,2,0,1:T(8,128)S(1)}, ...), branch_computations={%region_1.1_spmd, %region_2.2_spmd.clone} | conditional | flops 3223781376 | bytes 23593088 | solution.py:101
  77.7 1.7 fusion.9
  79.4 1.1 dynamic-slice_select_fusion
  84.8 1.6 multiply_subtract_fusion
  90.0 0.6 convolution_add_fusion
  92.9 2.0 subtract_bitcast_fusion
  95.1 4.5 %dynamic_update_slice.5 = f32[2,1,256,512]{3,2,0,1:T(8,128)S(1)} dynamic-update-slice(f32[2,1,256,512]{3,2,0,1:T(8,128)S(1)} %get-tuple-element.615, f32[2,1,256,256]{3,2,0,1:T(8,128)S(1)} %fusion.8, s32[]{:T(128)} %constant.73.clone.1, s32[]{:T(128)} %constant.73.clone.1, s32[]{:T(128)} %constant.73.clone.1, s32[]{:T(128)S(6)} %select_n.117) | dynamic-update-slice | bytes 1048580 | tf_op jit(solution)/shard_map/while/body/eval_jaxpr/cond/branch_1_fun/dynamic_update_slice | solution.py:87
  99.7 1.3 collective-permute-start
  101.2 2.3 collective-permute-done
  103.5 0.8 copy-done
  104.5 9.7 %reduce-scatter.2.cloned.1.call-done = f32[2,128,256]{2,1,0:T(8,128)} async-done(((f32[2,256,256]{2,1,0:T(8,128)}), f32[2,128,256]{2,1,0:T(8,128)}) %reduce-scatter.2.cloned.1.call-update) | async-done | bytes 262160 | tf_op jit(solution)/shard_map/reduce_scatter | solution.py:118
  114.2 8.5 %collective-permute-done.2 = f32[2,1,256,256]{3,2,1,0:T(8,128)S(1)} collective-permute-done((f32[2,1,256,256]{3,2,1,0:T(8,128)S(1)}, f32[2,1,256,256]{3,2,1,0:T(8,128)S(1)}, u32[]{:S(2)}, u32[]{:S(2)}) %collective-permute-start.2) | collective-permute-done | bytes 524320 | tf_op jit(solution)/shard_map/ppermute | solution.py:12
  122.6 0.9 slice_add_fusion
  123.5 104.6 %all-reduce.2.cloned.1.call-done = f32[2,128,256]{2,1,0:T(8,128)} async-done(((f32[2,128,256]{2,1,0:T(8,128)}), f32[2,128,256]{2,1,0:T(8,128)}) %all-reduce.2.cloned.1.call-update) | async-done | bytes 262160 | tf_op jit(solution)/shard_map/psum | solution.py:119
  228.1 1.7 copy.32
  (58 shorter events, 18.7 us)
Async XLA Ops:
  7.2 18.5 %copy-start.1 = (f32[2,1,256,256]{3,2,1,0:T(8,128)S(1)}, f32[2,1,256,256]{3,2,1,0:T(8,128)}, u32[]{:S(2)}) copy-start(f32[2,1,256,256]{3,2,1,0:T(8,128)} %param.10) | copy-start | bytes 1572868
  7.2 107.0 %reduce-scatter.2.cloned.1.call-start = ((), (), s32[]{:S(2)}) async-start(), calls=%async_computation.1 | async-start | bytes 786432 | tf_op jit(solution)/shard_map/reduce_scatter | solution.py:118
  7.2 18.5 %collective-permute-start.1 = (f32[2,1,256,256]{3,2,1,0:T(8,128)}, f32[2,1,256,256]{3,2,1,0:T(8,128)S(1)}, u32[]{:S(2)}, u32[]{:S(2)}) collective-permute-start(f32[2,1,256,256]{3,2,1,0:T(8,128)} %param.10), channel_id=1, source_target_pairs={{0,30},{2,0},{4,2},{6,4},{8,6},{10,8},{12,10},{14,12},{16,14},{18,... | collective-permute-start | bytes 1572872 | tf_op jit(solution)/shard_map/ppermute | solution.py:12
  27.0 0.7 copy-start.2
  27.9 23.6 %collective-permute-start = (f32[2,1,256,256]{3,2,0,1:T(8,128)S(1)}, f32[2,1,256,256]{3,2,0,1:T(8,128)S(1)}, u32[]{:S(2)}, u32[]{:S(2)}) collective-permute-start(f32[2,1,256,256]{3,2,0,1:T(8,128)S(1)} %pad_maximum_fusion.3), channel_id=1, source_target_pairs={{1,0},{3,2},{5,4},{7,6},{9,8},{11,10},{13,12},{15,14},{17,16},{19,... | collective-permute-start | bytes 1572872 | tf_op jit(solution)/shard_map/while/body/eval_jaxpr/ppermute | solution.py:18
  73.7 3.8 %collective-permute-start = (f32[2,1,256,256]{3,2,0,1:T(8,128)S(1)}, f32[2,1,256,256]{3,2,0,1:T(8,128)S(1)}, u32[]{:S(2)}, u32[]{:S(2)}) collective-permute-start(f32[2,1,256,256]{3,2,0,1:T(8,128)S(1)} %pad_maximum_fusion.3), channel_id=1, source_target_pairs={{1,0},{3,2},{5,4},{7,6},{9,8},{11,10},{13,12},{15,14},{17,16},{19,... | collective-permute-start | bytes 1572872 | tf_op jit(solution)/shard_map/while/body/eval_jaxpr/ppermute | solution.py:18
  99.7 3.8 %collective-permute-start = (f32[2,1,256,256]{3,2,0,1:T(8,128)S(1)}, f32[2,1,256,256]{3,2,0,1:T(8,128)S(1)}, u32[]{:S(2)}, u32[]{:S(2)}) collective-permute-start(f32[2,1,256,256]{3,2,0,1:T(8,128)S(1)} %pad_maximum_fusion.3), channel_id=1, source_target_pairs={{1,0},{3,2},{5,4},{7,6},{9,8},{11,10},{13,12},{15,14},{17,16},{19,... | collective-permute-start | bytes 1572872 | tf_op jit(solution)/shard_map/while/body/eval_jaxpr/ppermute | solution.py:18
  103.5 0.8 copy-start
  104.3 123.8 %all-reduce.2.cloned.1.call-start = ((), (), s32[]{:S(2)}) async-start(), calls=%async_computation.2 | async-start | bytes 524288 | tf_op jit(solution)/shard_map/psum | solution.py:119
  104.4 18.2 %collective-permute-start.2 = (f32[2,1,256,256]{3,2,1,0:T(8,128)S(1)}, f32[2,1,256,256]{3,2,1,0:T(8,128)S(1)}, u32[]{:S(2)}, u32[]{:S(2)}) collective-permute-start(f32[2,1,256,256]{3,2,1,0:T(8,128)S(1)} %slice.61), channel_id=1, source_target_pairs={{0,2},{2,4},{4,6},{6,8},{8,10},{10,12},{12,14},{14,16},{16,18},{18... | collective-permute-start | bytes 1572872 | tf_op jit(solution)/shard_map/ppermute | solution.py:12
Sparse Core Ops, SparseCore 0:
  104.4 9.6 reduce-scatter.1
  120.2 107.8 all-reduce.1
where the time goes:
time: 237 us
  waiting for transfers between devices  158 us (67%)
  matrix products  23.8 us (10%)
  local copies, waits for them, and re-layouts  16 us (7%)
  between operations  14.1 us (6%)
  starting transfers between devices  11 us (5%)
  other arithmetic  9.15 us (4%)
  loops' own time  4.03 us (2%)
    psum x1, waiting for transfers between devices, shards(): probe_grad = lax.psum(probe_band, 'lat')  105 us
    ppermute x3, waiting for transfers between devices, shifted(): lax.ppermute(value, axis, [(source, source + steps) for source in range(f...  26.7 us
    ppermute x2, waiting for transfers between devices, from_behind(): return lax.ppermute(value, axis, pairs)  17.5 us
    dot_general x16, matrix products, right_product(): jnp.einsum('bjk,kl->bjl', field, table, precision=lax.Precision.HIGHEST)  14.3 us
    reduce_scatter x1, waiting for transfers between devices, shards(): lax.psum_scatter(probe_sum, 'depth', scatter_dimension=1, tiled=True)  9.68 us
    dot_general x16, matrix products, left_product(): jnp.einsum('jk,bkl->bjl', table, field, precision=lax.Precision.HIGHEST)  9.54 us
    dynamic_update_slice x2, local copies, waits for them, and re-layouts, run_section(): lax.dynamic_update_slice(grad_buffer, current + addition, corner)  8.99 us
    ppermute x2, starting transfers between devices, from_behind(): return lax.ppermute(value, axis, pairs)  7.04 us
  transfers between devices with their start and end apart: 7, of which 7 were waited for; matrix products, arithmetic and copies ran while one was open for 2% of the time, Pallas kernels for 0%

commit v1 on v0

v1 whole, which is shorter than its diff:
```python
import functools
import math

import jax
import jax.numpy as jnp
import ml_dtypes
import numpy as np
from jax import lax
from jax.experimental import pallas as pl
from jax.experimental.pallas import tpu as pltpu
from jax.sharding import PartitionSpec as P

F32 = jnp.float32
BF16 = jnp.bfloat16
MESH_ID = pl.DeviceIdType.MESH


def dft_tables(length):
    index = np.arange(length)
    angles = (index[:, None] * index[None, :] % length) * (2.0 * math.pi / length)
    re, im = np.cos(angles) / math.sqrt(length), -np.sin(angles) / math.sqrt(length)
    left = np.block([[re, -im], [im, re]])
    high = left.astype(ml_dtypes.bfloat16)
    low = (left - high.astype(np.float64)).astype(ml_dtypes.bfloat16)
    return np.stack([high, low, high.T, low.T])


def cos_sin(phase):
    half = phase * 0.5
    sq = half * half
    sin_half = half * (1.0 + sq * (-1 / 6 + sq * (1 / 120 + sq * (-1 / 5040 + sq * (1 / 362880 + sq * (-1 / 39916800 + sq * (1 / 6227020800)))))))
    cos_half = 1.0 + sq * (-1 / 2 + sq * (1 / 24 + sq * (-1 / 720 + sq * (1 / 40320 + sq * (-1 / 3628800 + sq * (1 / 479001600 + sq * (-1 / 87178291200)))))))
    return 1.0 - 2.0 * sin_half * sin_half, 2.0 * sin_half * cos_half


def dot(a, b):
    return jnp.dot(a, b, preferred_element_type=F32)


def kernel(
    lat_size, depth_size, reduce_inside,
    obj_hbm, saved_hbm, cot_hbm, phase_hbm, tab_hbm, off_ref,
    grad_ref, probe_ref,
    obj, psi, cot, phase, tab, halo, wave, gout, ah, al, bh, bl, cosr, sinr,
    over, over_in, gsum, band, slots, mine, final,
    lsem, halo_s, halo_r, over_s, over_r, wave_s, wave_r, band_s, band_r, rs_s, rs_r, ag_s, ag_r,
):
    width = obj.shape[2]
    count = psi.shape[1]
    lat = lax.axis_index("lat")
    depth = lax.axis_index("depth")
    left = lax.rem(lat + lat_size - 1, lat_size)
    right = lax.rem(lat + 1, lat_size)
    last = depth == depth_size - 1

    loads = [
        pltpu.make_async_copy(source, target, lsem.at[n])
        for n, (source, target) in enumerate(
            ((phase_hbm, phase), (cot_hbm, cot), (tab_hbm, tab), (saved_hbm, psi), (obj_hbm, obj))
        )
    ]
    for load in loads:
        load.start()

    barrier = pltpu.get_barrier_semaphore()
    for k in range(1, lat_size):
        pl.semaphore_signal(barrier, inc=1, device_id=(lax.rem(lat + k, lat_size), depth), device_id_type=MESH_ID)
    for k in range(1, depth_size):
        pl.semaphore_signal(barrier, inc=1, device_id=(lat, lax.rem(depth + k, depth_size)), device_id_type=MESH_ID)
    pl.semaphore_wait(barrier, lat_size - 1 + depth_size - 1)

    halo_copy = pltpu.make_async_remote_copy(
        src_ref=obj_hbm, dst_ref=halo, send_sem=halo_s, recv_sem=halo_r,
        device_id=(left, depth), device_id_type=MESH_ID,
    )
    halo_copy.start()

    loads[0].wait()
    cosr[...], sinr[...] = cos_sin(phase[...])
    loads[1].wait()

    @pl.when(last)
    def _():
        for p in range(count):
            for c in range(2):
                wave[c, p] = pltpu.roll(cot[c, p], off_ref[p], 1)

    loads[2].wait()
    loads[3].wait()
    for p in range(count):
        for c in range(2):
            psi[c, p, 0] = pltpu.roll(psi[c, p, 0], off_ref[p], 1)

    wave_copy = pltpu.make_async_remote_copy(
        src_ref=gout, dst_ref=wave, send_sem=wave_s, recv_sem=wave_r,
        device_id=(lat, lax.rem(depth + depth_size - 1, depth_size)), device_id_type=MESH_ID,
    )

    @pl.when(depth < depth_size - 1)
    def _():
        wave_copy.wait_recv()

    def put(high_ref, low_ref, row, col, block):
        rows, cols = pl.ds(row * width, width), pl.ds(col * width, width)
        high = block.astype(BF16)
        high_ref[rows, cols] = high
        low_ref[rows, cols] = (block - high.astype(F32)).astype(BF16)

    def block_of(n, size=1):
        return pl.ds(n * width, size * width)

    def left_block(high, low, row, col, src_h, src_l):
        r, c = block_of(row), block_of(col)
        return dot(tab[high, r, :], src_h[:, c]) + (dot(tab[high, r, :], src_l[:, c]) + dot(tab[low, r, :], src_h[:, c]))

    def right_block(high, low, row, col, src_h, src_l):
        r, c = block_of(row), block_of(col)
        return dot(src_h[r, :], tab[high, :, c]) + (dot(src_l[r, :], tab[high, :, c]) + dot(src_h[r, :], tab[low, :, c]))

    for p in range(count):
        for c in range(2):
            put(ah, al, c, p, wave[c, p])
    for p in range(count):
        for c in range(2):
            put(bh, bl, p, c, left_block(0, 1, c, p, ah, al))
    for p in range(count):
        re = right_block(2, 3, p, 0, bh, bl)
        im = right_block(2, 3, p, 1, bh, bl)
        put(bh, bl, p, 0, re * cosr[...] + im * sinr[...])
        put(bh, bl, p, 1, im * cosr[...] - re * sinr[...])
    for p in range(count):
        for c in range(2):
            put(ah, al, c, p, right_block(0, 1, p, c, bh, bl))
    column = lax.broadcasted_iota(jnp.int32, (width, width), 1)
    for p in range(count):
        re = left_block(2, 3, 0, p, ah, al)
        im = left_block(2, 3, 1, p, ah, al)
        wave[0, p] = re
        wave[1, p] = im
        own = column >= off_ref[p]
        saved_re, saved_im = psi[0, p, 0], psi[1, p, 0]
        delta = (saved_re * re + saved_im * im, saved_re * im - saved_im * re)
        for c in range(2):
            if p == 0:
                grad_ref[c, 0] = jnp.where(own, delta[c], 0.0)
                over[c] = jnp.where(own, 0.0, delta[c])
            else:
                grad_ref[c, 0] += jnp.where(own, delta[c], 0.0)
                over[c] += jnp.where(own, 0.0, delta[c])
    over_copy = pltpu.make_async_remote_copy(
        src_ref=over, dst_ref=over_in, send_sem=over_s, recv_sem=over_r,
        device_id=(right, depth), device_id_type=MESH_ID,
    )
    over_copy.start()

    loads[4].wait()
    halo_copy.wait_recv()
    for p in range(count):
        own = column >= off_ref[p]
        trans_re = jnp.where(own, obj[0, 0], halo[0, 0])
        trans_im = jnp.where(own, obj[1, 0], halo[1, 0])
        re, im = wave[0, p], wave[1, p]
        gout[0, p] = trans_re * re + trans_im * im
        gout[1, p] = trans_re * im - trans_im * re

    @pl.when(depth > 0)
    def _():
        wave_copy.start()

    @pl.when(depth == 0)
    def _():
        for c in range(2):
            total = pltpu.roll(gout[c, 0], width - off_ref[0], 1)
            for p in range(1, count):
                total = total + pltpu.roll(gout[c, p], width - off_ref[p], 1)
            gsum[c] = total

    if reduce_inside:
        rows = width // depth_size
        piece = rows // lat_size

        def band_copy(r):
            return pltpu.make_async_remote_copy(
                src_ref=gsum.at[:, pl.ds(r * rows, rows), :], dst_ref=band, send_sem=band_s.at[r], recv_sem=band_r,
                device_id=(lat, r), device_id_type=MESH_ID,
            )

        @pl.when(depth == 0)
        def _():
            for r in range(1, depth_size):
                band_copy(r).start()
            band[...] = gsum[:, :rows, :]

        @pl.when(depth > 0)
        def _():
            band_copy(1).wait_recv()

        def part(n):
            return pl.ds(pl.multiple_of(n * piece, piece), piece)

        scatter, gather = [], []
        for k in range(1, lat_size):
            peer = lax.rem(lat + k, lat_size)
            scatter.append(pltpu.make_async_remote_copy(
                src_ref=band.at[:, part(peer), :], dst_ref=slots.at[k], send_sem=rs_s.at[k], recv_sem=rs_r.at[k],
                device_id=(peer, depth), device_id_type=MESH_ID,
            ))
            gather.append(pltpu.make_async_remote_copy(
                src_ref=mine, dst_ref=final.at[:, part(lat), :], send_sem=ag_s.at[k], recv_sem=ag_r.at[k],
                device_id=(peer, depth), device_id_type=MESH_ID,
            ))
        for copy in scatter:
            copy.start()
        total = band[:, part(lat), :]
        for k, copy in enumerate(scatter):
            copy.wait_recv()
            total = total + slots[k + 1]
        mine[...] = total
        for copy in gather:
            copy.start()
        final[:, part(lat), :] = total

    over_copy.wait_recv()
    grad_ref[:, 0] += over_in[...]

    if reduce_inside:
        for copy in gather:
            copy.wait_recv()
        probe_ref[...] = final[...]
        for copy in scatter + gather:
            copy.wait_send()

        @pl.when(depth == 0)
        def _():
            for r in range(1, depth_size):
                band_copy(r).wait_send()
    else:
        probe_ref[...] = jnp.zeros_like(probe_ref)

        @pl.when(depth == 0)
        def _():
            probe_ref[...] = gsum[...]

    @pl.when(depth > 0)
    def _():
        wave_copy.wait_send()

    halo_copy.wait_send()
    over_copy.wait_send()


def shards(lat_size, depth_size, saved_waves, object_slices, cotangent, transfer_phase, offsets):
    width = object_slices.shape[2]
    count = offsets.shape[0]
    reduce_inside = width % (8 * depth_size * lat_size) == 0
    rows = width // depth_size if reduce_inside else width
    piece = max(8, rows // lat_size)
    tables = jnp.asarray(dft_tables(width))
    anywhere = pl.BlockSpec(memory_space=pl.ANY)
    field = pltpu.VMEM((2, count, width, width), F32)
    plane = pltpu.VMEM((2, width, width), F32)
    a_part = pltpu.VMEM((2 * width, count * width), BF16)
    b_part = pltpu.VMEM((count * width, 2 * width), BF16)
    table = pltpu.VMEM((width, width), F32)
    dma = pltpu.SemaphoreType.DMA
    grad, probe = pl.pallas_call(
        functools.partial(kernel, lat_size, depth_size, reduce_inside),
        out_shape=(
            jax.ShapeDtypeStruct(object_slices.shape, F32),
            jax.ShapeDtypeStruct((2, rows, width), F32),
        ),
        in_specs=[anywhere] * 5 + [pl.BlockSpec(memory_space=pltpu.SMEM)],
        out_specs=(pl.BlockSpec(memory_space=pltpu.VMEM),) * 2,
        scratch_shapes=[
            pltpu.VMEM(object_slices.shape, F32),
            pltpu.VMEM(saved_waves.shape, F32),
            field,
            table,
            pltpu.VMEM(tables.shape, BF16),
            pltpu.VMEM(object_slices.shape, F32),
            field,
            field,
            a_part, a_part, b_part, b_part,
            table, table,
            plane, plane, plane,
            pltpu.VMEM((2, rows, width), F32),
            pltpu.VMEM((lat_size, 2, piece, width), F32),
            pltpu.VMEM((2, piece, width), F32),
            pltpu.VMEM((2, rows, width), F32),
            dma((5,)), dma, dma, dma, dma, dma, dma, dma((depth_size,)), dma,
            dma((lat_size,)), dma((lat_size,)), dma((lat_size,)), dma((lat_size,)),
        ],
        compiler_params=pltpu.CompilerParams(
            collective_id=0, has_side_effects=True, vmem_limit_bytes=40 * 1024 * 1024
        ),
        name="ptycho_backward",
    )(object_slices, saved_waves, cotangent, transfer_phase, tables, offsets)
    if not reduce_inside:
        probe = lax.psum(lax.psum_scatter(probe, "depth", scatter_dimension=1, tiled=True), "lat")
    return grad, probe


def solution(mesh):
    placed = (
        P(None, "lat", "depth", None, None),
        P(None, "depth", None, "lat"),
        P(None, "lat", None, None),
        P(),
        P("lat"),
    )
    return jax.shard_map(
        functools.partial(shards, mesh.shape["lat"], mesh.shape["depth"]),
        mesh=mesh,
        in_specs=placed,
        out_specs=(P(None, "depth", None, "lat"), P(None, "depth", None)),
        check_vma=False,
    )
```

time: 237 us -> 56 us (0.24)
  waiting for transfers between devices: 158 us -> 0 us
  Pallas kernels: 0 us -> 46.9 us
  matrix products: 23.8 us -> 0 us
  between operations: 14.1 us -> 0.65 us
  starting transfers between devices: 11 us -> 0 us
  other arithmetic: 9.15 us -> 0 us
  local copies, waits for them, and re-layouts: 16 us -> 8.18 us
  loops' own time: 4.03 us -> 0 us
    psum x1 -> x0, waiting for transfers between devices: 105 us -> none  [shards(): probe_grad = lax.psum(probe_band, 'lat')]
    pallas_call x0 -> x1, Pallas kernels: none -> 46.9 us  [shards(): pl.pallas_call(functools.partial(kernel, lat_size, depth_size, reduce_ins...]
    ppermute x5 -> x0, waiting for transfers between devices: 44.2 us -> none  [the longest x3 26.7 us: shifted(): lax.ppermute(value, axis, [(source, source + steps) for source in range(f...]
    dot_general x32 -> x0, matrix products: 23.8 us -> none  [the longest x16 14.3 us: right_product(): jnp.einsum('bjk,kl->bjl', field, table, precision=lax.Precision.HIGHEST)]
    ppermute x5 -> x0, starting transfers between devices: 10.9 us -> none  [the longest x2 7.04 us: from_behind(): return lax.ppermute(value, axis, pairs)]
    reduce_scatter x1 -> x0, waiting for transfers between devices: 9.68 us -> none  [shards(): lax.psum_scatter(probe_sum, 'depth', scatter_dimension=1, tiled=True)]
    dynamic_update_slice x2 -> x0, local copies, waits for them, and re-layouts: 8.99 us -> none  [run_section(): lax.dynamic_update_slice(grad_buffer, current + addition, corner)]
    unnamed x7 -> x14, local copies, waits for them, and re-layouts: 3.08 us -> 8.18 us
  transfers between devices with their start and end apart: 7 -> 0, of which waited for: 7 -> 0; matrix products, arithmetic and copies ran while one was open for 2% -> 0% of each run, Pallas kernels for 0% -> 0%
where the time goes in v1:
time: 56 us; the launch traced here: 55.7 us
  Pallas kernels  46.9 us (84%)
  local copies, waits for them, and re-layouts  8.18 us (15%)
  between operations  0.65 us (1%)
    pallas_call x1, Pallas kernels, shards(): pl.pallas_call(functools.partial(kernel, lat_size, depth_size, reduce_ins...  46.9 us
    unnamed x14, local copies, waits for them, and re-layouts  8.18 us

profile of v1, /device:TPU:0, one launch (start us, length us, event | category | flops | bytes accessed | tf_op | source)
XLA Modules:
  0.0 55.7 jit_solution(916757898220162100)
XLA Ops:
  0.6 0.0 copy-start
  0.6 1.6 %copy-done = bf16[4,512,512]{2,1,0:T(8,128)(2,1)S(1)} copy-done((bf16[4,512,512]{2,1,0:T(8,128)(2,1)S(1)}, bf16[4,512,512]{2,1,0:T(8,128)(2,1)}, u32[]{:S(2)}) %copy-start) | copy-done | bytes 2097176
  2.2 0.0 copy-start.1
  2.2 1.2 %copy-done.1 = f32[2,2,1,256,256]{4,3,2,1,0:T(8,128)S(1)} copy-done((f32[2,2,1,256,256]{4,3,2,1,0:T(8,128)S(1)}, f32[2,2,1,256,256]{4,3,2,1,0:T(8,128)}, u32[]{:S(2)}) %copy-start.1) | copy-done | bytes 1048600
  3.5 0.0 copy-start.2
  3.5 1.2 %copy-done.2 = f32[2,2,256,256]{3,2,1,0:T(8,128)S(1)} copy-done((f32[2,2,256,256]{3,2,1,0:T(8,128)S(1)}, f32[2,2,256,256]{3,2,1,0:T(8,128)}, u32[]{:S(2)}) %copy-start.2) | copy-done | bytes 1048600
  4.7 0.0 copy-start.3
  4.7 1.0 %copy-done.3 = f32[2,1,256,256]{3,2,1,0:T(8,128)S(1)} copy-done((f32[2,1,256,256]{3,2,1,0:T(8,128)S(1)}, f32[2,1,256,256]{3,2,1,0:T(8,128)}, u32[]{:S(2)}) %copy-start.3) | copy-done | bytes 524312
  5.7 0.0 copy-start.4
  5.7 0.9 %copy-done.4 = f32[256,256]{1,0:T(8,128)S(1)} copy-done((f32[256,256]{1,0:T(8,128)S(1)}, f32[256,256]{1,0:T(8,128)}, u32[]{:S(2)}) %copy-start.4) | copy-done | bytes 262168
  6.7 0.0 copy-start.5
  6.7 0.7 %copy-done.5 = s32[2]{0:T(128)S(1)} copy-done((s32[2]{0:T(128)S(1)}, s32[2]{0:T(128)}, u32[]{:S(2)}) %copy-start.5) | copy-done | bytes 32
  7.3 46.9 %ptycho_backward.1 = (f32[2,1,256,256]{3,2,1,0:T(8,128)S(1)}, f32[2,128,256]{2,1,0:T(8,128)S(1)}) custom-call(f32[2,1,256,256]{3,2,1,0:T(8,128)S(1)} %copy-done.3, f32[2,2,1,256,256]{4,3,2,1,0:T(8,128)S(1)} %copy-done.1, f32[2,2,256,256]{3,2,1,0:T(8,128)S(1)} %copy-done.2, f32[256,256]{1,0:T(8,128)S(1)} %copy-done.4, bf16[4,512,512]{2,1,0:T(8,128)(2,1)S(1)} %copy-done, ...), custom_call_target="tpu_custom_call" | custom-call | tf_op jit(solution)/shard_map/ptycho_backward/pallas_call | solution.py:266
  54.2 0.8 %copy.10 = f32[2,1,256,256]{3,2,1,0:T(8,128)} copy(f32[2,1,256,256]{3,2,1,0:T(8,128)S(1)} %get-tuple-element.4) | data formatting | bytes 1048576
  55.0 0.7 %copy.11 = f32[2,128,256]{2,1,0:T(8,128)} copy(f32[2,128,256]{2,1,0:T(8,128)S(1)} %get-tuple-element.5) | data formatting | bytes 524288
Async XLA Ops:
  0.6 1.6 %copy-start = (bf16[4,512,512]{2,1,0:T(8,128)(2,1)S(1)}, bf16[4,512,512]{2,1,0:T(8,128)(2,1)}, u32[]{:S(2)}) copy-start(bf16[4,512,512]{2,1,0:T(8,128)(2,1)} %constant.2.clone.tab_hbm) | copy-start | bytes 6291460
  2.2 1.2 %copy-start.1 = (f32[2,2,1,256,256]{4,3,2,1,0:T(8,128)S(1)}, f32[2,2,1,256,256]{4,3,2,1,0:T(8,128)}, u32[]{:S(2)}) copy-start(f32[2,2,1,256,256]{4,3,2,1,0:T(8,128)} %saved_hbm.1) | copy-start | bytes 3145732
  3.5 1.2 %copy-start.2 = (f32[2,2,256,256]{3,2,1,0:T(8,128)S(1)}, f32[2,2,256,256]{3,2,1,0:T(8,128)}, u32[]{:S(2)}) copy-start(f32[2,2,256,256]{3,2,1,0:T(8,128)} %cot_hbm.1) | copy-start | bytes 3145732
  4.7 1.0 %copy-start.3 = (f32[2,1,256,256]{3,2,1,0:T(8,128)S(1)}, f32[2,1,256,256]{3,2,1,0:T(8,128)}, u32[]{:S(2)}) copy-start(f32[2,1,256,256]{3,2,1,0:T(8,128)} %obj_hbm.1) | copy-start | bytes 1572868
  5.7 0.9 %copy-start.4 = (f32[256,256]{1,0:T(8,128)S(1)}, f32[256,256]{1,0:T(8,128)}, u32[]{:S(2)}) copy-start(f32[256,256]{1,0:T(8,128)} %phase_hbm.1) | copy-start | bytes 786436
  6.7 0.7 %copy-start.5 = (s32[2]{0:T(128)S(1)}, s32[2]{0:T(128)}, u32[]{:S(2)}) copy-start(s32[2]{0:T(128)} %off_ref.1) | copy-start | bytes 28

commit v2 on v1

--- a/solution.py
+++ b/solution.py
@@ -13,6 +13,8 @@
 F32 = jnp.float32
 BF16 = jnp.bfloat16
 MESH_ID = pl.DeviceIdType.MESH
+CHUNKS = 4
+SCHEDULE = ((0, 4, 0, 0), (4, 0, 0, 0))
 
 
 def dft_tables(length):
@@ -42,8 +44,8 @@
     obj_hbm, saved_hbm, cot_hbm, phase_hbm, tab_hbm, off_ref,
     grad_ref, probe_ref,
     obj, psi, cot, phase, tab, halo, wave, gout, ah, al, bh, bl, cosr, sinr,
-    over, over_in, gsum, band, slots, mine, final,
-    lsem, halo_s, halo_r, over_s, over_r, wave_s, wave_r, band_s, band_r, rs_s, rs_r, ag_s, ag_r,
+    over, over_in, gsum, band, slots, mine, paired, total_out, final,
+    lsem, halo_s, halo_r, over_s, over_r, wave_s, wave_r, band_s, band_r, rs_s, rs_r, ag_s, ag_r, pair_s, pair_r, halo_go, over_go,
 ):
     width = obj.shape[2]
     count = psi.shape[1]
@@ -73,7 +75,10 @@
         src_ref=obj_hbm, dst_ref=halo, send_sem=halo_s, recv_sem=halo_r,
         device_id=(left, depth), device_id_type=MESH_ID,
     )
-    halo_copy.start()
+
+    @pl.when(last)
+    def _():
+        halo_copy.start()
 
     loads[0].wait()
     cosr[...], sinr[...] = cos_sin(phase[...])
@@ -91,14 +96,26 @@
         for c in range(2):
             psi[c, p, 0] = pltpu.roll(psi[c, p, 0], off_ref[p], 1)
 
-    wave_copy = pltpu.make_async_remote_copy(
-        src_ref=gout, dst_ref=wave, send_sem=wave_s, recv_sem=wave_r,
-        device_id=(lat, lax.rem(depth + depth_size - 1, depth_size)), device_id_type=MESH_ID,
-    )
+    wave_copies = [
+        pltpu.make_async_remote_copy(
+            src_ref=gout.at[:, p], dst_ref=wave.at[:, p], send_sem=wave_s.at[p], recv_sem=wave_r.at[p],
+            device_id=(lat, lax.rem(depth + depth_size - 1, depth_size)), device_id_type=MESH_ID,
+        )
+        for p in range(count)
+    ]
+
+    above, below = (lat, lax.rem(depth + 1, depth_size)), (lat, lax.rem(depth + depth_size - 1, depth_size))
 
     @pl.when(depth < depth_size - 1)
     def _():
-        wave_copy.wait_recv()
+        pl.semaphore_wait(halo_go, 1)
+        halo_copy.start()
+        halo_copy.wait_send()
+        pl.semaphore_signal(over_go, inc=1, device_id=above, device_id_type=MESH_ID)
+
+        @pl.when(depth > 0)
+        def _():
+            pl.semaphore_signal(halo_go, inc=1, device_id=below, device_id_type=MESH_ID)
 
     def put(high_ref, low_ref, row, col, block):
         rows, cols = pl.ds(row * width, width), pl.ds(col * width, width)
@@ -117,22 +134,22 @@
         r, c = block_of(row), block_of(col)
         return dot(src_h[r, :], tab[high, :, c]) + (dot(src_l[r, :], tab[high, :, c]) + dot(src_h[r, :], tab[low, :, c]))
 
+    column = lax.broadcasted_iota(jnp.int32, (width, width), 1)
     for p in range(count):
+        @pl.when(depth < depth_size - 1)
+        def _(p=p):
+            wave_copies[p].wait_recv()
+
         for c in range(2):
             put(ah, al, c, p, wave[c, p])
-    for p in range(count):
         for c in range(2):
             put(bh, bl, p, c, left_block(0, 1, c, p, ah, al))
-    for p in range(count):
         re = right_block(2, 3, p, 0, bh, bl)
         im = right_block(2, 3, p, 1, bh, bl)
         put(bh, bl, p, 0, re * cosr[...] + im * sinr[...])
         put(bh, bl, p, 1, im * cosr[...] - re * sinr[...])
-    for p in range(count):
         for c in range(2):
             put(ah, al, c, p, right_block(0, 1, p, c, bh, bl))
-    column = lax.broadcasted_iota(jnp.int32, (width, width), 1)
-    for p in range(count):
         re = left_block(2, 3, 0, p, ah, al)
         im = left_block(2, 3, 1, p, ah, al)
         wave[0, p] = re
@@ -147,11 +164,39 @@
             else:
                 grad_ref[c, 0] += jnp.where(own, delta[c], 0.0)
                 over[c] += jnp.where(own, 0.0, delta[c])
-    over_copy = pltpu.make_async_remote_copy(
-        src_ref=over, dst_ref=over_in, send_sem=over_s, recv_sem=over_r,
-        device_id=(right, depth), device_id_type=MESH_ID,
-    )
-    over_copy.start()
+    chunk = width // CHUNKS
+    over_copies = [
+        pltpu.make_async_remote_copy(
+            src_ref=over.at[:, pl.ds(n * chunk, chunk), :], dst_ref=over_in.at[:, pl.ds(n * chunk, chunk), :],
+            send_sem=over_s.at[n], recv_sem=over_r.at[n], device_id=(right, depth), device_id_type=MESH_ID,
+        )
+        for n in range(CHUNKS)
+    ]
+    plan = SCHEDULE if reduce_inside else ((CHUNKS, 0, 0, 0),) * 2
+
+    def send_over(point, front):
+        first = sum(plan[1 - front][:point])
+        for copy in over_copies[first:first + plan[1 - front][point]]:
+            copy.start()
+
+    def send_over_both(point):
+        @pl.when(depth == 0)
+        def _():
+            send_over(point, 1)
+
+        @pl.when(depth > 0)
+        def _():
+            send_over(point, 0)
+
+    @pl.when(depth == 0)
+    def _():
+        send_over(0, 1)
+
+    @pl.when(last)
+    def _():
+        halo_copy.wait_send()
+        if depth_size > 1:
+            pl.semaphore_signal(halo_go, inc=1, device_id=below, device_id_type=MESH_ID)
 
     loads[4].wait()
     halo_copy.wait_recv()
@@ -163,9 +208,14 @@
         gout[0, p] = trans_re * re + trans_im * im
         gout[1, p] = trans_re * im - trans_im * re
 
+        @pl.when(depth > 0)
+        def _(p=p):
+            wave_copies[p].start()
+
     @pl.when(depth > 0)
     def _():
-        wave_copy.start()
+        pl.semaphore_wait(over_go, 1)
+        send_over(0, 0)
 
     @pl.when(depth == 0)
     def _():
@@ -177,7 +227,8 @@
 
     if reduce_inside:
         rows = width // depth_size
-        piece = rows // lat_size
+        lanes = lat_size // 2
+        piece = rows // lanes
 
         def band_copy(r):
             return pltpu.make_async_remote_copy(
@@ -198,36 +249,50 @@
         def part(n):
             return pl.ds(pl.multiple_of(n * piece, piece), piece)
 
+        rank, parity = lat // 2, lax.rem(lat, 2)
+        pair = pltpu.make_async_remote_copy(
+            src_ref=mine, dst_ref=paired, send_sem=pair_s, recv_sem=pair_r,
+            device_id=(lat + 1 - 2 * parity, depth), device_id_type=MESH_ID,
+        )
         scatter, gather = [], []
-        for k in range(1, lat_size):
-            peer = lax.rem(lat + k, lat_size)
+        for k in range(1, lanes):
+            slot = lax.rem(rank + k, lanes)
+            peer = 2 * slot + parity
             scatter.append(pltpu.make_async_remote_copy(
-                src_ref=band.at[:, part(peer), :], dst_ref=slots.at[k], send_sem=rs_s.at[k], recv_sem=rs_r.at[k],
+                src_ref=band.at[:, part(slot), :], dst_ref=slots.at[k], send_sem=rs_s.at[k], recv_sem=rs_r.at[k],
                 device_id=(peer, depth), device_id_type=MESH_ID,
             ))
             gather.append(pltpu.make_async_remote_copy(
-                src_ref=mine, dst_ref=final.at[:, part(lat), :], send_sem=ag_s.at[k], recv_sem=ag_r.at[k],
+                src_ref=total_out, dst_ref=final.at[:, part(rank), :], send_sem=ag_s.at[k], recv_sem=ag_r.at[k],
                 device_id=(peer, depth), device_id_type=MESH_ID,
             ))
         for copy in scatter:
             copy.start()
-        total = band[:, part(lat), :]
+        send_over_both(1)
+        total = band[:, part(rank), :]
         for k, copy in enumerate(scatter):
             copy.wait_recv()
             total = total + slots[k + 1]
         mine[...] = total
+        pair.start()
+        send_over_both(2)
+        pair.wait_recv()
+        total = total + paired[...]
+        total_out[...] = total
         for copy in gather:
             copy.start()
-        final[:, part(lat), :] = total
-
-    over_copy.wait_recv()
-    grad_ref[:, 0] += over_in[...]
+        send_over_both(3)
+        final[:, part(rank), :] = total
+
+    for n, copy in enumerate(over_copies):
+        copy.wait_recv()
+        grad_ref[:, 0, n * chunk:(n + 1) * chunk, :] += over_in[:, n * chunk:(n + 1) * chunk, :]
 
     if reduce_inside:
         for copy in gather:
             copy.wait_recv()
         probe_ref[...] = final[...]
-        for copy in scatter + gather:
+        for copy in scatter + gather + [pair]:
             copy.wait_send()
 
         @pl.when(depth == 0)
@@ -243,18 +308,19 @@
 
     @pl.when(depth > 0)
     def _():
-        wave_copy.wait_send()
-
-    halo_copy.wait_send()
-    over_copy.wait_send()
+        for copy in wave_copies:
+            copy.wait_send()
+
+    for copy in over_copies:
+        copy.wait_send()
 
 
 def shards(lat_size, depth_size, saved_waves, object_slices, cotangent, transfer_phase, offsets):
     width = object_slices.shape[2]
     count = offsets.shape[0]
-    reduce_inside = width % (8 * depth_size * lat_size) == 0
+    reduce_inside = lat_size % 2 == 0 and width % (4 * depth_size * lat_size) == 0
     rows = width // depth_size if reduce_inside else width
-    piece = max(8, rows // lat_size)
+    piece = max(8, 2 * rows // lat_size)
     tables = jnp.asarray(dft_tables(width))
     anywhere = pl.BlockSpec(memory_space=pl.ANY)
     field = pltpu.VMEM((2, count, width, width), F32)
@@ -286,12 +352,15 @@
             pltpu.VMEM((2, rows, width), F32),
             pltpu.VMEM((lat_size, 2, piece, width), F32),
             pltpu.VMEM((2, piece, width), F32),
+            pltpu.VMEM((2, piece, width), F32),
+            pltpu.VMEM((2, piece, width), F32),
             pltpu.VMEM((2, rows, width), F32),
-            dma((5,)), dma, dma, dma, dma, dma, dma, dma((depth_size,)), dma,
-            dma((lat_size,)), dma((lat_size,)), dma((lat_size,)), dma((lat_size,)),
+            dma((5,)), dma, dma, dma((CHUNKS,)), dma((CHUNKS,)), dma((count,)), dma((count,)), dma((depth_size,)), dma,
+            dma((lat_size,)), dma((lat_size,)), dma((lat_size,)), dma((lat_size,)), dma, dma,
+            pltpu.SemaphoreType.REGULAR, pltpu.SemaphoreType.REGULAR,
         ],
         compiler_params=pltpu.CompilerParams(
-            collective_id=0, has_side_effects=True, vmem_limit_bytes=40 * 1024 * 1024
+            collective_id=0, has_side_effects=True, vmem_limit_bytes=60 * 1024 * 1024
         ),
         name="ptycho_backward",
     )(object_slices, saved_waves, cotangent, transfer_phase, tables, offsets)

time: 56 us -> 51.5 us (0.920)
  local copies, waits for them, and re-layouts: 8.18 us -> 3.54 us
    unnamed x14 -> x2, local copies, waits for them, and re-layouts: 8.18 us -> 3.54 us
where the time goes in v2:
time: 51.5 us; the launch traced here: 51 us
  Pallas kernels  46.8 us (91%)
  local copies, waits for them, and re-layouts  3.54 us (7%)
  between operations  0.64 us (1%)
    pallas_call x1, Pallas kernels, shards(): pl.pallas_call(functools.partial(kernel, lat_size, depth_size, reduce_ins...  46.8 us
    unnamed x2, local copies, waits for them, and re-layouts  3.54 us

profile of v2, /device:TPU:0, one launch (start us, length us, event | category | flops | bytes accessed | tf_op | source)
XLA Modules:
  0.0 51.0 jit_solution(5987869796478779639)
XLA Ops:
  0.6 46.8 %ptycho_backward.1 = (f32[2,1,256,256]{3,2,1,0:T(8,128)}, f32[2,128,256]{2,1,0:T(8,128)}) custom-call(f32[2,1,256,256]{3,2,1,0:T(8,128)} %obj_hbm.1, f32[2,2,1,256,256]{4,3,2,1,0:T(8,128)} %saved_hbm.1, f32[2,2,256,256]{3,2,1,0:T(8,128)} %cot_hbm.1, f32[256,256]{1,0:T(8,128)} %phase_hbm.1, bf16[4,512,512]{2,1,0:T(8,128)(2,1)} %constant.2.clone.tab_hbm, s32[2]{0:T(128)} %off_ref.1), custom_call_target="tpu_custom_call" | custom-call | tf_op jit(solution)/shard_map/ptycho_backward/pallas_call | solution.py:332
  47.4 1.9 %copy.10 = f32[2,1,256,256]{3,2,1,0:T(8,128)} copy(f32[2,1,256,256]{3,2,1,0:T(8,128)} %get-tuple-element.4) | data formatting | bytes 1048576
  49.3 1.7 %copy.11 = f32[2,128,256]{2,1,0:T(8,128)} copy(f32[2,128,256]{2,1,0:T(8,128)} %get-tuple-element.5) | data formatting | bytes 524288
